TPU v7x, 128 devices: a whole 4x4x4 slice. The times are simulated.
128 devices in a mesh: row: 16 (over z_hi, y, core), col: 8 (over x, z_lo).
Axes of the slice: x: 4, y: 4, z: 4 (z_hi: 2, z_lo: 2; z = z_hi * 2 + z_lo), core: 2. Of those that a mesh axis runs over, the one named last changes fastest.
Arguments:
- vectors_in: float32 [16384, 16384], P('row', 'col'), may hold values from -6 to 6
- reflectors: float32 [8, 128, 128], P(None, 'row', 'col'), may hold values from -6 to 6
- offsets: int32 [8], replicated, may hold values from 1 to 64, as said below
Outputs:
- vectors_out: float32 [16384, 16384], P('row', 'col')
Inputs may be any that keep to these rules, and one draw needn't show every extreme that they name: `offsets`: each sweep's first window begins within the first half of a reflector's length; the values 1 and 64 both occur in every draw.
All inputs are finite; a program needn't handle non-finite values.
Results may differ from a plain program's by a relative error of at most 0.0002.
Values sent between devices are 32-bit elements; how exact they have to be, the bound alone decides.
A program may use at most 128 MiB of HBM per device.

v0:
```python
import jax
import jax.numpy as jnp
from jax import lax
from jax.sharding import PartitionSpec as P

B = 128
SWEEPS = 8


def passed_along(block, axis, distance):
    devices = range(lax.axis_size(axis))
    route = [(i - distance, i) for i in devices if i - distance in devices]
    return lax.ppermute(block, axis, route)


def reflect(block, vecs, first_row, total_rows):
    count = vecs.shape[0]
    width = vecs.shape[1]
    index = first_row + jnp.arange(count * width, dtype=jnp.int32).reshape(count, width)
    vecs = jnp.where((index >= 0) & (index < total_rows), vecs, jnp.float32(0.0))
    scale = 2.0 / (jnp.sum(vecs * vecs, axis=1) + 1e-06)
    tiles = block.reshape(count, width, -1)
    coeff = jnp.einsum("kb,kbc->kc", vecs, tiles, precision=lax.Precision.HIGHEST) * scale[:, None]
    return (tiles - vecs[:, :, None] * coeff[:, None, :]).reshape(count * width, -1)


def body(vectors_in, reflectors, offsets):
    rank = lax.axis_index("row")
    local_rows = vectors_in.shape[0]
    total = local_rows * lax.axis_size("row")
    half = B // 2
    matrix = vectors_in
    for sweep in range(SWEEPS):
        start = offsets[sweep]
        vecs = lax.all_gather(reflectors[sweep], "col", axis=1, tiled=True)
        below = passed_along(matrix[:half], "row", -1)
        extended = jnp.concatenate([matrix, below], axis=0)
        window = lax.dynamic_slice_in_dim(extended, start, local_rows, 0)
        window = reflect(window, vecs, rank * local_rows + start, total)
        extended = lax.dynamic_update_slice_in_dim(extended, window, start, 0)
        returned = passed_along(extended[local_rows:], "row", 1)
        row_ids = jnp.arange(half, dtype=jnp.int32)[:, None]
        leading = jnp.where((row_ids < start) & (rank > 0), returned, extended[:half])
        matrix = jnp.concatenate([leading, extended[half:local_rows]], axis=0)
    return matrix


def solution(mesh):
    in_specs = (P("row", "col"), P(None, "row", "col"), P())
    out_specs = P("row", "col")
    return jax.shard_map(body, mesh=mesh, in_specs=in_specs, out_specs=out_specs, check_vma=False)
```

profile of v0, /device:TPU:25, one launch (start us, length us, event | category | flops | bytes accessed | tf_op | source)
XLA Modules:
  0.0 763.2 jit_solution(7260054649428667113)
XLA Ops:
  6.8 22.0 %all-gather = f32[1,8,128]{1,0,2:T(1,128)S(1)} all-gather(f32[1,8,16]{1,0,2:T(1,128)S(1)} %copy.44), channel_id=2, replica_groups=mesh['row'=16,'col'=8] {'col'}, dimensions={2}, use_global_device_ids=true | all-gather | bytes 4608 | tf_op jit(solution)/shard_map/all_gather | solution.py:35
  46.1 21.9 %dynamic_update_slice.24 = f32[1088,2048]{1,0:T(8,128)} dynamic-update-slice(f32[1088,2048]{1,0:T(8,128)} %copy-done, f32[1024,2048]{1,0:T(8,128)} %fusion.7, s32[]{:T(128)S(6)} %select_n.82, s32[]{:T(128)} %constant.5.clone.1) | dynamic-update-slice | bytes 16777220 | tf_op jit(solution)/shard_map/dynamic_update_slice | solution.py:40
  69.1 13.3 %collective-permute-start.1 = (f32[64,2048]{1,0:T(8,128)S(1)}, f32[64,2048]{1,0:T(8,128)S(1)}, u32[]{:S(2)}, u32[]{:S(2)}) collective-permute-start(f32[64,2048]{1,0:T(8,128)S(1)} %slice.164), channel_id=1, source_target_pairs={{0,8},{8,16},{16,24},{24,32},{32,40},{40,48},{48,56},{56,64},{64,7... | collective-permute-start | bytes 1572872 | tf_op jit(solution)/shard_map/ppermute | solution.py:13
  93.4 22.1 %all-gather.1 = f32[1,8,128]{1,0,2:T(1,128)S(1)} all-gather(f32[1,8,16]{1,0,2:T(1,128)S(1)} %copy.45), channel_id=3, replica_groups=mesh['row'=16,'col'=8] {'col'}, dimensions={2}, use_global_device_ids=true | all-gather | bytes 4608 | tf_op jit(solution)/shard_map/all_gather | solution.py:35
  132.3 8.1 %fusion.6 = f32[1024,2048]{1,0:T(8,128)} fusion(f32[8,2048]{1,0:T(8,128)S(1)} %bitcast_multiply_fusion.14, f32[1024]{0:T(1024)S(1)} %bitcast.147, f32[1088,2048]{1,0:T(8,128)} %pad_maximum_fusion, s32[]{:T(128)S(6)} %select_n.85), kind=kLoop, calls=%fused_computation.21 | loop fusion | flops 4194304 | bytes 16846852 | tf_op jit(solution)/shard_map/sub | solution.py:24
  140.4 21.9 %dynamic_update_slice.25 = f32[1088,2048]{1,0:T(8,128)} dynamic-update-slice(f32[1088,2048]{1,0:T(8,128)} %pad_maximum_fusion, f32[1024,2048]{1,0:T(8,128)} %fusion.6, s32[]{:T(128)S(6)} %select_n.85, s32[]{:T(128)} %constant.5.clone.1) | dynamic-update-slice | bytes 16777220 | tf_op jit(solution)/shard_map/dynamic_update_slice | solution.py:40
  163.4 14.3 %collective-permute-start.3 = (f32[64,2048]{1,0:T(8,128)S(1)}, f32[64,2048]{1,0:T(8,128)S(1)}, u32[]{:S(2)}, u32[]{:S(2)}) collective-permute-start(f32[64,2048]{1,0:T(8,128)S(1)} %slice.167), channel_id=1, source_target_pairs={{0,8},{8,16},{16,24},{24,32},{32,40},{40,48},{48,56},{56,64},{64,7... | collective-permute-start | bytes 1572872 | tf_op jit(solution)/shard_map/ppermute | solution.py:13
  188.9 22.1 %all-gather.2 = f32[1,8,128]{1,0,2:T(1,128)S(1)} all-gather(f32[1,8,16]{1,0,2:T(1,128)S(1)} %copy.46), channel_id=4, replica_groups=mesh['row'=16,'col'=8] {'col'}, dimensions={2}, use_global_device_ids=true | all-gather | bytes 4608 | tf_op jit(solution)/shard_map/all_gather | solution.py:35
  227.9 8.1 %fusion.5 = f32[1024,2048]{1,0:T(8,128)} fusion(f32[8,2048]{1,0:T(8,128)S(1)} %bitcast_multiply_fusion.13, f32[1024]{0:T(1024)S(1)} %bitcast.149, f32[1088,2048]{1,0:T(8,128)} %pad_maximum_fusion.1, s32[]{:T(128)S(6)} %select_n.88), kind=kLoop, calls=%fused_computation.19 | loop fusion | flops 4194304 | bytes 16846852 | tf_op jit(solution)/shard_map/sub | solution.py:24
  236.0 21.9 %dynamic_update_slice.26 = f32[1088,2048]{1,0:T(8,128)} dynamic-update-slice(f32[1088,2048]{1,0:T(8,128)} %pad_maximum_fusion.1, f32[1024,2048]{1,0:T(8,128)} %fusion.5, s32[]{:T(128)S(6)} %select_n.88, s32[]{:T(128)} %constant.5.clone.1) | dynamic-update-slice | bytes 16777220 | tf_op jit(solution)/shard_map/dynamic_update_slice | solution.py:40
  259.0 14.5 %collective-permute-start.5 = (f32[64,2048]{1,0:T(8,128)S(1)}, f32[64,2048]{1,0:T(8,128)S(1)}, u32[]{:S(2)}, u32[]{:S(2)}) collective-permute-start(f32[64,2048]{1,0:T(8,128)S(1)} %slice.170), channel_id=1, source_target_pairs={{0,8},{8,16},{16,24},{24,32},{32,40},{40,48},{48,56},{56,64},{64,7... | collective-permute-start | bytes 1572872 | tf_op jit(solution)/shard_map/ppermute | solution.py:13
  274.1 5.6 collective-permute-done.5
  285.0 22.6 %all-gather.3 = f32[1,8,128]{1,0,2:T(1,128)S(1)} all-gather(f32[1,8,16]{1,0,2:T(1,128)S(1)} %copy.47), channel_id=5, replica_groups=mesh['row'=16,'col'=8] {'col'}, dimensions={2}, use_global_device_ids=true | all-gather | bytes 4608 | tf_op jit(solution)/shard_map/all_gather | solution.py:35
  324.6 8.1 %fusion.4 = f32[1024,2048]{1,0:T(8,128)} fusion(f32[8,2048]{1,0:T(8,128)S(1)} %bitcast_multiply_fusion.12, f32[1024]{0:T(1024)S(1)} %bitcast.151, f32[1088,2048]{1,0:T(8,128)} %pad_maximum_fusion.2, s32[]{:T(128)S(6)} %select_n.91), kind=kLoop, calls=%fused_computation.17 | loop fusion | flops 4194304 | bytes 16846852 | tf_op jit(solution)/shard_map/sub | solution.py:24
  332.7 21.9 %dynamic_update_slice.27 = f32[1088,2048]{1,0:T(8,128)} dynamic-update-slice(f32[1088,2048]{1,0:T(8,128)} %pad_maximum_fusion.2, f32[1024,2048]{1,0:T(8,128)} %fusion.4, s32[]{:T(128)S(6)} %select_n.91, s32[]{:T(128)} %constant.5.clone.1) | dynamic-update-slice | bytes 16777220 | tf_op jit(solution)/shard_map/dynamic_update_slice | solution.py:40
  355.6 14.1 %collective-permute-start.7 = (f32[64,2048]{1,0:T(8,128)S(1)}, f32[64,2048]{1,0:T(8,128)S(1)}, u32[]{:S(2)}, u32[]{:S(2)}) collective-permute-start(f32[64,2048]{1,0:T(8,128)S(1)} %slice.173), channel_id=1, source_target_pairs={{0,8},{8,16},{16,24},{24,32},{32,40},{40,48},{48,56},{56,64},{64,7... | collective-permute-start | bytes 1572872 | tf_op jit(solution)/shard_map/ppermute | solution.py:13
  381.0 22.2 %all-gather.4 = f32[1,8,128]{1,0,2:T(1,128)S(1)} all-gather(f32[1,8,16]{1,0,2:T(1,128)S(1)} %copy.48), channel_id=6, replica_groups=mesh['row'=16,'col'=8] {'col'}, dimensions={2}, use_global_device_ids=true | all-gather | bytes 4608 | tf_op jit(solution)/shard_map/all_gather | solution.py:35
  420.1 8.1 %fusion.3 = f32[1024,2048]{1,0:T(8,128)} fusion(f32[8,2048]{1,0:T(8,128)S(1)} %bitcast_multiply_fusion.11, f32[1024]{0:T(1024)S(1)} %bitcast.153, f32[1088,2048]{1,0:T(8,128)} %pad_maximum_fusion.3, s32[]{:T(128)S(6)} %select_n.94), kind=kLoop, calls=%fused_computation.15 | loop fusion | flops 4194304 | bytes 16846852 | tf_op jit(solution)/shard_map/sub | solution.py:24
  428.2 21.8 %dynamic_update_slice.28 = f32[1088,2048]{1,0:T(8,128)} dynamic-update-slice(f32[1088,2048]{1,0:T(8,128)} %pad_maximum_fusion.3, f32[1024,2048]{1,0:T(8,128)} %fusion.3, s32[]{:T(128)S(6)} %select_n.94, s32[]{:T(128)} %constant.5.clone.1) | dynamic-update-slice | bytes 16777220 | tf_op jit(solution)/shard_map/dynamic_update_slice | solution.py:40
  451.1 14.3 %collective-permute-start.9 = (f32[64,2048]{1,0:T(8,128)S(1)}, f32[64,2048]{1,0:T(8,128)S(1)}, u32[]{:S(2)}, u32[]{:S(2)}) collective-permute-start(f32[64,2048]{1,0:T(8,128)S(1)} %slice.176), channel_id=1, source_target_pairs={{0,8},{8,16},{16,24},{24,32},{32,40},{40,48},{48,56},{56,64},{64,7... | collective-permute-start | bytes 1572872 | tf_op jit(solution)/shard_map/ppermute | solution.py:13
  476.4 22.0 %all-gather.5 = f32[1,8,128]{1,0,2:T(1,128)S(1)} all-gather(f32[1,8,16]{1,0,2:T(1,128)S(1)} %copy.49), channel_id=7, replica_groups=mesh['row'=16,'col'=8] {'col'}, dimensions={2}, use_global_device_ids=true | all-gather | bytes 4608 | tf_op jit(solution)/shard_map/all_gather | solution.py:35
  515.2 8.1 %fusion.2 = f32[1024,2048]{1,0:T(8,128)} fusion(f32[8,2048]{1,0:T(8,128)S(1)} %bitcast_multiply_fusion.10, f32[1024]{0:T(1024)S(1)} %bitcast.155, f32[1088,2048]{1,0:T(8,128)} %pad_maximum_fusion.4, s32[]{:T(128)S(6)} %select_n.97), kind=kLoop, calls=%fused_computation.13 | loop fusion | flops 4194304 | bytes 16846852 | tf_op jit(solution)/shard_map/sub | solution.py:24
  523.2 21.3 %dynamic_update_slice.29 = f32[1088,2048]{1,0:T(8,128)} dynamic-update-slice(f32[1088,2048]{1,0:T(8,128)} %pad_maximum_fusion.4, f32[1024,2048]{1,0:T(8,128)} %fusion.2, s32[]{:T(128)S(6)} %select_n.97, s32[]{:T(128)} %constant.5.clone.1) | dynamic-update-slice | bytes 16777220 | tf_op jit(solution)/shard_map/dynamic_update_slice | solution.py:40
  545.7 14.5 %collective-permute-start.11 = (f32[64,2048]{1,0:T(8,128)S(1)}, f32[64,2048]{1,0:T(8,128)S(1)}, u32[]{:S(2)}, u32[]{:S(2)}) collective-permute-start(f32[64,2048]{1,0:T(8,128)S(1)} %slice.179), channel_id=1, source_target_pairs={{0,8},{8,16},{16,24},{24,32},{32,40},{40,48},{48,56},{56,64},{64,7... | collective-permute-start | bytes 1572872 | tf_op jit(solution)/shard_map/ppermute | solution.py:13
  571.2 22.3 %all-gather.6 = f32[1,8,128]{1,0,2:T(1,128)S(1)} all-gather(f32[1,8,16]{1,0,2:T(1,128)S(1)} %copy.50), channel_id=8, replica_groups=mesh['row'=16,'col'=8] {'col'}, dimensions={2}, use_global_device_ids=true | all-gather | bytes 4608 | tf_op jit(solution)/shard_map/all_gather | solution.py:35
  610.4 8.1 %fusion.1 = f32[1024,2048]{1,0:T(8,128)} fusion(f32[8,2048]{1,0:T(8,128)S(1)} %bitcast_multiply_fusion.9, f32[1024]{0:T(1024)S(1)} %bitcast.157, f32[1088,2048]{1,0:T(8,128)} %pad_maximum_fusion.5, s32[]{:T(128)S(6)} %select_n.100), kind=kLoop, calls=%fused_computation.11 | loop fusion | flops 4194304 | bytes 16846852 | tf_op jit(solution)/shard_map/sub | solution.py:24
  618.5 21.8 %dynamic_update_slice.30 = f32[1088,2048]{1,0:T(8,128)} dynamic-update-slice(f32[1088,2048]{1,0:T(8,128)} %pad_maximum_fusion.5, f32[1024,2048]{1,0:T(8,128)} %fusion.1, s32[]{:T(128)S(6)} %select_n.100, s32[]{:T(128)} %constant.5.clone.1) | dynamic-update-slice | bytes 16777220 | tf_op jit(solution)/shard_map/dynamic_update_slice | solution.py:40
  641.3 14.2 %collective-permute-start.13 = (f32[64,2048]{1,0:T(8,128)S(1)}, f32[64,2048]{1,0:T(8,128)S(1)}, u32[]{:S(2)}, u32[]{:S(2)}) collective-permute-start(f32[64,2048]{1,0:T(8,128)S(1)} %slice.182), channel_id=1, source_target_pairs={{0,8},{8,16},{16,24},{24,32},{32,40},{40,48},{48,56},{56,64},{64,7... | collective-permute-start | bytes 1572872 | tf_op jit(solution)/shard_map/ppermute | solution.py:13
  666.9 22.1 %all-gather.7 = f32[1,8,128]{1,0,2:T(1,128)S(1)} all-gather(f32[1,8,16]{1,0,2:T(1,128)S(1)} %copy.51), channel_id=9, replica_groups=mesh['row'=16,'col'=8] {'col'}, dimensions={2}, use_global_device_ids=true | all-gather | bytes 4608 | tf_op jit(solution)/shard_map/all_gather | solution.py:35
  705.9 8.1 %fusion = f32[1024,2048]{1,0:T(8,128)} fusion(f32[8,2048]{1,0:T(8,128)S(1)} %bitcast_multiply_fusion.8, f32[1024]{0:T(1024)S(1)} %bitcast.159, f32[1088,2048]{1,0:T(8,128)} %pad_maximum_fusion.6, s32[]{:T(128)S(6)} %select_n.103), kind=kLoop, calls=%fused_computation.9 | loop fusion | flops 4194304 | bytes 16846852 | tf_op jit(solution)/shard_map/sub | solution.py:24
  714.0 21.9 %dynamic_update_slice.31 = f32[1088,2048]{1,0:T(8,128)} dynamic-update-slice(f32[1088,2048]{1,0:T(8,128)} %pad_maximum_fusion.6, f32[1024,2048]{1,0:T(8,128)} %fusion, s32[]{:T(128)S(6)} %select_n.103, s32[]{:T(128)} %constant.5.clone.1) | dynamic-update-slice | bytes 16777220 | tf_op jit(solution)/shard_map/dynamic_update_slice | solution.py:40
  737.0 14.4 %collective-permute-start.15 = (f32[64,2048]{1,0:T(8,128)S(1)}, f32[64,2048]{1,0:T(8,128)S(1)}, u32[]{:S(2)}, u32[]{:S(2)}) collective-permute-start(f32[64,2048]{1,0:T(8,128)S(1)} %slice.185), channel_id=1, source_target_pairs={{0,8},{8,16},{16,24},{24,32},{32,40},{40,48},{48,56},{56,64},{64,7... | collective-permute-start | bytes 1572872 | tf_op jit(solution)/shard_map/ppermute | solution.py:13
  (131 shorter events, 214.6 us)
Async XLA Ops:
  1.1 34.4 %collective-permute-start = (f32[64,2048]{1,0:T(8,128)S(1)}, f32[64,2048]{1,0:T(8,128)S(1)}, u32[]{:S(2)}, u32[]{:S(2)}) collective-permute-start(f32[64,2048]{1,0:T(8,128)S(1)} %slice.131), channel_id=1, source_target_pairs={{8,0},{16,8},{24,16},{32,24},{40,32},{48,40},{56,48},{64,56},{72,6... | collective-permute-start | bytes 1572872 | tf_op jit(solution)/shard_map/ppermute | solution.py:13
  35.6 6.0 copy-start
  69.1 19.5 %collective-permute-start.1 = (f32[64,2048]{1,0:T(8,128)S(1)}, f32[64,2048]{1,0:T(8,128)S(1)}, u32[]{:S(2)}, u32[]{:S(2)}) collective-permute-start(f32[64,2048]{1,0:T(8,128)S(1)} %slice.164), channel_id=1, source_target_pairs={{0,8},{8,16},{16,24},{24,32},{32,40},{40,48},{48,56},{56,64},{64,7... | collective-permute-start | bytes 1572872 | tf_op jit(solution)/shard_map/ppermute | solution.py:13
  89.8 30.3 %collective-permute-start.2 = (f32[64,2048]{1,0:T(8,128)S(1)}, f32[64,2048]{1,0:T(8,128)S(1)}, u32[]{:S(2)}, u32[]{:S(2)}) collective-permute-start(f32[64,2048]{1,0:T(8,128)S(1)} %slice_select_fusion.7), channel_id=1, source_target_pairs={{8,0},{16,8},{24,16},{32,24},{40,32},{48,40},{56,48},{64,56},{72,6... | collective-permute-start | bytes 1572872 | tf_op jit(solution)/shard_map/ppermute | solution.py:13
  163.4 20.5 %collective-permute-start.3 = (f32[64,2048]{1,0:T(8,128)S(1)}, f32[64,2048]{1,0:T(8,128)S(1)}, u32[]{:S(2)}, u32[]{:S(2)}) collective-permute-start(f32[64,2048]{1,0:T(8,128)S(1)} %slice.167), channel_id=1, source_target_pairs={{0,8},{8,16},{16,24},{24,32},{32,40},{40,48},{48,56},{56,64},{64,7... | collective-permute-start | bytes 1572872 | tf_op jit(solution)/shard_map/ppermute | solution.py:13
  185.1 30.5 %collective-permute-start.4 = (f32[64,2048]{1,0:T(8,128)S(1)}, f32[64,2048]{1,0:T(8,128)S(1)}, u32[]{:S(2)}, u32[]{:S(2)}) collective-permute-start(f32[64,2048]{1,0:T(8,128)S(1)} %slice_select_fusion.6), channel_id=1, source_target_pairs={{8,0},{16,8},{24,16},{32,24},{40,32},{48,40},{56,48},{64,56},{72,6... | collective-permute-start | bytes 1572872 | tf_op jit(solution)/shard_map/ppermute | solution.py:13
  259.0 20.8 %collective-permute-start.5 = (f32[64,2048]{1,0:T(8,128)S(1)}, f32[64,2048]{1,0:T(8,128)S(1)}, u32[]{:S(2)}, u32[]{:S(2)}) collective-permute-start(f32[64,2048]{1,0:T(8,128)S(1)} %slice.170), channel_id=1, source_target_pairs={{0,8},{8,16},{16,24},{24,32},{32,40},{40,48},{48,56},{56,64},{64,7... | collective-permute-start | bytes 1572872 | tf_op jit(solution)/shard_map/ppermute | solution.py:13
  280.9 31.3 %collective-permute-start.6 = (f32[64,2048]{1,0:T(8,128)S(1)}, f32[64,2048]{1,0:T(8,128)S(1)}, u32[]{:S(2)}, u32[]{:S(2)}) collective-permute-start(f32[64,2048]{1,0:T(8,128)S(1)} %slice_select_fusion.5), channel_id=1, source_target_pairs={{8,0},{16,8},{24,16},{32,24},{40,32},{48,40},{56,48},{64,56},{72,6... | collective-permute-start | bytes 1572872 | tf_op jit(solution)/shard_map/ppermute | solution.py:13
  355.6 20.3 %collective-permute-start.7 = (f32[64,2048]{1,0:T(8,128)S(1)}, f32[64,2048]{1,0:T(8,128)S(1)}, u32[]{:S(2)}, u32[]{:S(2)}) collective-permute-start(f32[64,2048]{1,0:T(8,128)S(1)} %slice.173), channel_id=1, source_target_pairs={{0,8},{8,16},{16,24},{24,32},{32,40},{40,48},{48,56},{56,64},{64,7... | collective-permute-start | bytes 1572872 | tf_op jit(solution)/shard_map/ppermute | solution.py:13
  377.1 30.8 %collective-permute-start.8 = (f32[64,2048]{1,0:T(8,128)S(1)}, f32[64,2048]{1,0:T(8,128)S(1)}, u32[]{:S(2)}, u32[]{:S(2)}) collective-permute-start(f32[64,2048]{1,0:T(8,128)S(1)} %slice_select_fusion.4), channel_id=1, source_target_pairs={{8,0},{16,8},{24,16},{32,24},{40,32},{48,40},{56,48},{64,56},{72,6... | collective-permute-start | bytes 1572872 | tf_op jit(solution)/shard_map/ppermute | solution.py:13
  451.1 20.5 %collective-permute-start.9 = (f32[64,2048]{1,0:T(8,128)S(1)}, f32[64,2048]{1,0:T(8,128)S(1)}, u32[]{:S(2)}, u32[]{:S(2)}) collective-permute-start(f32[64,2048]{1,0:T(8,128)S(1)} %slice.176), channel_id=1, source_target_pairs={{0,8},{8,16},{16,24},{24,32},{32,40},{40,48},{48,56},{56,64},{64,7... | collective-permute-start | bytes 1572872 | tf_op jit(solution)/shard_map/ppermute | solution.py:13
  472.7 30.2 %collective-permute-start.10 = (f32[64,2048]{1,0:T(8,128)S(1)}, f32[64,2048]{1,0:T(8,128)S(1)}, u32[]{:S(2)}, u32[]{:S(2)}) collective-permute-start(f32[64,2048]{1,0:T(8,128)S(1)} %slice_select_fusion.3), channel_id=1, source_target_pairs={{8,0},{16,8},{24,16},{32,24},{40,32},{48,40},{56,48},{64,56},{72,6... | collective-permute-start | bytes 1572872 | tf_op jit(solution)/shard_map/ppermute | solution.py:13
  523.2 47.9 %copy-start.2 = (f32[1,8,16]{2,1,0:T(8,128)S(1)}, f32[1,8,16]{2,1,0:T(8,128)}, u32[]{:S(2)}) copy-start(f32[1,8,16]{2,1,0:T(8,128)} %get-tuple-element.22) | copy-start | bytes 1540
  545.7 20.7 %collective-permute-start.11 = (f32[64,2048]{1,0:T(8,128)S(1)}, f32[64,2048]{1,0:T(8,128)S(1)}, u32[]{:S(2)}, u32[]{:S(2)}) collective-permute-start(f32[64,2048]{1,0:T(8,128)S(1)} %slice.179), channel_id=1, source_target_pairs={{0,8},{8,16},{16,24},{24,32},{32,40},{40,48},{48,56},{56,64},{64,7... | collective-permute-start | bytes 1572872 | tf_op jit(solution)/shard_map/ppermute | solution.py:13
  567.5 30.5 %collective-permute-start.12 = (f32[64,2048]{1,0:T(8,128)S(1)}, f32[64,2048]{1,0:T(8,128)S(1)}, u32[]{:S(2)}, u32[]{:S(2)}) collective-permute-start(f32[64,2048]{1,0:T(8,128)S(1)} %slice_select_fusion.2), channel_id=1, source_target_pairs={{8,0},{16,8},{24,16},{32,24},{40,32},{48,40},{56,48},{64,56},{72,6... | collective-permute-start | bytes 1572872 | tf_op jit(solution)/shard_map/ppermute | solution.py:13
  618.4 48.4 %copy-start.1 = (f32[1,8,16]{2,1,0:T(8,128)S(1)}, f32[1,8,16]{2,1,0:T(8,128)}, u32[]{:S(2)}) copy-start(f32[1,8,16]{2,1,0:T(8,128)} %get-tuple-element.21) | copy-start | bytes 1540
  641.3 20.3 %collective-permute-start.13 = (f32[64,2048]{1,0:T(8,128)S(1)}, f32[64,2048]{1,0:T(8,128)S(1)}, u32[]{:S(2)}, u32[]{:S(2)}) collective-permute-start(f32[64,2048]{1,0:T(8,128)S(1)} %slice.182), channel_id=1, source_target_pairs={{0,8},{8,16},{16,24},{24,32},{32,40},{40,48},{48,56},{56,64},{64,7... | collective-permute-start | bytes 1572872 | tf_op jit(solution)/shard_map/ppermute | solution.py:13
  662.8 30.8 %collective-permute-start.14 = (f32[64,2048]{1,0:T(8,128)S(1)}, f32[64,2048]{1,0:T(8,128)S(1)}, u32[]{:S(2)}, u32[]{:S(2)}) collective-permute-start(f32[64,2048]{1,0:T(8,128)S(1)} %slice_select_fusion.1), channel_id=1, source_target_pairs={{8,0},{16,8},{24,16},{32,24},{40,32},{48,40},{56,48},{64,56},{72,6... | collective-permute-start | bytes 1572872 | tf_op jit(solution)/shard_map/ppermute | solution.py:13
  737.0 20.5 %collective-permute-start.15 = (f32[64,2048]{1,0:T(8,128)S(1)}, f32[64,2048]{1,0:T(8,128)S(1)}, u32[]{:S(2)}, u32[]{:S(2)}) collective-permute-start(f32[64,2048]{1,0:T(8,128)S(1)} %slice.185), channel_id=1, source_target_pairs={{0,8},{8,16},{16,24},{24,32},{32,40},{40,48},{48,56},{56,64},{64,7... | collective-permute-start | bytes 1572872 | tf_op jit(solution)/shard_map/ppermute | solution.py:13
where the time goes:
time: 779 us; the launch traced here: 763 us
  local copies, waits for them, and re-layouts  255 us (33%)
  blocking collectives  177 us (23%)
  starting transfers between devices  130 us (17%)
  other arithmetic  107 us (14%)
  waiting for transfers between devices  40.6 us (5%)
  matrix products  32.3 us (4%)
  between operations  20.7 us (3%)
    all_gather x8, blocking collectives, body(): vecs = lax.all_gather(reflectors[sweep], 'col', axis=1, tiled=True)  177 us
    dynamic_update_slice x8, local copies, waits for them, and re-layouts, body(): extended = lax.dynamic_update_slice_in_dim(extended, window, start, 0)  174 us
    ppermute x16, starting transfers between devices, passed_along(): return lax.ppermute(block, axis, route)  130 us
    sub x8, other arithmetic, reflect(): tiles - vecs[:, :, None] * coeff[:, None, :]  61.2 us
    ppermute x16, waiting for transfers between devices, passed_along(): return lax.ppermute(block, axis, route)  40.6 us
    dynamic_slice x8, local copies, waits for them, and re-layouts, body(): window = lax.dynamic_slice_in_dim(extended, start, local_rows, 0)  32.6 us
    dot_general x8, matrix products, reflect(): jnp.einsum('kb,kbc->kc', vecs, tiles, precision=lax.Precision.HIGHEST)  32.3 us
    slice x8, local copies, waits for them, and re-layouts, body(): matrix = jnp.concatenate([leading, extended[half:local_rows]], axis=0)  30.2 us
  transfers between devices with their start and end apart: 16, of which 8 were waited for; matrix products, arithmetic and copies ran while one was open for 6% of the time, Pallas kernels for 0%

commit v1 on v0

v1 whole, which is shorter than its diff:
```python
import functools

import jax
import jax.numpy as jnp
from jax import lax
from jax.experimental import pallas as pl
from jax.experimental.pallas import tpu as pltpu
from jax.sharding import PartitionSpec as P

MESH = pl.DeviceIdType.MESH
F32 = jnp.float32
BF16 = jnp.bfloat16
EPS = 1e-6
S = 8
W = 8
B = 128
N = 80
LAST = 64
MIB = 1 << 20


def exact_dot(a, b, dims):
    return lax.dot_general(
        a, b, (dims, ((), ())), precision=lax.Precision.HIGHEST, preferred_element_type=F32
    )


def split(x):
    hi = x.astype(BF16)
    return hi, (x - hi.astype(F32)).astype(BF16)


def iota(shape, axis):
    return lax.broadcasted_iota(jnp.int32, shape, axis)


def unit_inverse(n, row_s, col_s, eye):
    low = ((row_s // 2) == (col_s // 2)) & (row_s > col_s)
    inv = eye - jnp.where(low, n, 0.0)
    for b in (2, 4):
        low = ((row_s // (2 * b)) == (col_s // (2 * b))) & ((row_s // b) > (col_s // b))
        part = exact_dot(jnp.where(low, n, 0.0), inv, ((1,), (0,)))
        inv = inv - exact_dot(inv, part, ((1,), (0,)))
    return inv


def first_kernel(
    R, C, CHUNKS,
    off_ref, e_hbm, refl_hbm,
    e_ref, y_ref, c_ref,
    refl, mine, gat, hi_ref, lo_ref, vt, wt, p_ref, msg, near, recv,
    refl_sem, e_sem, out_sem, gat_sem, msg_sem, near_sem, p_sem, recv_sem,
):
    r = lax.axis_index("row")
    c = lax.axis_index("col")
    up = lax.rem(r + R - 1, R)
    down = lax.rem(r + 1, R)
    rows, cols = e_ref.shape
    step = rows // W
    width = cols // CHUNKS

    refl_copy = pltpu.make_async_copy(refl_hbm, refl, refl_sem)
    refl_copy.start()
    loads = []
    for i in range(W):
        part = pl.ds(i * step, step)
        load = pltpu.make_async_copy(e_hbm.at[part], e_ref.at[part], e_sem.at[i])
        load.start()
        loads.append(load)

    barrier = pltpu.get_barrier_semaphore()
    for d in range(1, C):
        pl.semaphore_signal(barrier, inc=1, device_id=(r, lax.rem(c + d, C)), device_id_type=MESH)
    for d in range(C):
        pl.semaphore_signal(barrier, inc=1, device_id=(up, lax.rem(c + d, C)), device_id_type=MESH)
    pl.semaphore_signal(barrier, inc=1, device_id=(down, c), device_id_type=MESH)

    refl_copy.wait()
    piece = refl.shape[2]
    tile = jnp.concatenate([refl[:, k, :] for k in range(W)], axis=1)
    mine[...] = tile
    gat[0, c] = tile
    pl.semaphore_wait(barrier, 2 * C)

    sends = []
    for d in range(1, C):
        sends.append(pltpu.make_async_remote_copy(
            src_ref=mine, dst_ref=gat.at[0, c], send_sem=out_sem.at[0, d], recv_sem=gat_sem.at[0, c],
            device_id=(r, lax.rem(c + d, C)), device_id_type=MESH))
    for d in range(C):
        sends.append(pltpu.make_async_remote_copy(
            src_ref=mine, dst_ref=gat.at[1, c], send_sem=out_sem.at[1, d], recv_sem=gat_sem.at[1, c],
            device_id=(down, lax.rem(c + d, C)), device_id_type=MESH))
    for copy in sends:
        copy.start()

    for i in range(W):
        loads[i].wait()

        @pl.loop(0, cols // 512)
        def _(j):
            at = (pl.ds(i * step, step), pl.ds(pl.multiple_of(j * 512, 512), 512))
            hi, lo = split(e_ref[at])
            hi_ref[at] = hi
            lo_ref[at] = lo

    for d in range(1, C):
        src = lax.rem(c + d, C)
        pltpu.make_async_remote_copy(
            src_ref=mine, dst_ref=gat.at[0, src], send_sem=out_sem.at[0, d], recv_sem=gat_sem.at[0, src],
            device_id=(r, src), device_id_type=MESH).wait_recv()
    for src in range(C):
        pltpu.make_async_remote_copy(
            src_ref=mine, dst_ref=gat.at[1, src], send_sem=out_sem.at[1, src], recv_sem=gat_sem.at[1, src],
            device_id=(up, src), device_id_type=MESH).wait_recv()

    lane = iota((S, B), 1)
    parts = [[gat[0, q] for q in range(C)], [gat[1, q] for q in range(C)]]

    def window(kind, k):
        out = jnp.zeros((S, B), F32)
        for q in range(C):
            turn = (q * piece - k * piece) % B
            x = parts[kind][q]
            x = x if turn == 0 else pltpu.roll(x, turn, 1)
            out = jnp.where((lane >= q * piece) & (lane < (q + 1) * piece), x, out)
        return out

    sub = iota((S, B), 0)
    off = jnp.zeros((S, B), jnp.int32)
    for s in range(S):
        off = jnp.where(sub == s, off_ref[s], off)

    vt[...] = jnp.zeros_like(vt)
    wt[...] = jnp.zeros_like(wt)
    tau_x = [None, None]
    for g in range(W + 1):
        x = window(1, W - 1) if g == 0 else window(0, g - 1)
        for b in range(7):
            x = jnp.where((off >> b) & 1 == 1, pltpu.roll(x, 1 << b, 1), x)
        here = jnp.where(lane >= off, x, 0.0)
        over = jnp.where(lane < off, x, 0.0)
        if g == 0:
            here = jnp.where(r > 0, here, 0.0)
            over = jnp.where(r > 0, over, 0.0)
        if g == W:
            over = jnp.where(r < R - 1, over, 0.0)
        square = here * here + over * over
        tau = 2.0 / (jnp.sum(square, axis=1, keepdims=True) + EPS)
        if g == 0:
            tau_x[0] = jnp.where(r > 0, tau, 0.0)
        if g == W:
            tau_x[1] = tau
        weight = 1.0 if g in (0, W) else tau
        rows_g = pl.ds(g * S, S)
        if g > 0:
            vt[rows_g, pl.ds((g - 1) * B, B)] = here
            wt[rows_g, pl.ds((g - 1) * B, B)] = here * weight
        if g < W:
            vt[rows_g, pl.ds(g * B, B)] = over
            wt[rows_g, pl.ds(g * B, B)] = over * weight

    ri, ci = iota((N, N), 0), iota((N, N), 1)
    row_s, col_s = ri % S, ci % S
    row_g, col_g = ri // S, ci // S
    eye = jnp.where(ri == ci, 1.0, 0.0).astype(F32)
    row_x = (row_g == 0) | (row_g == W)
    col_x = (col_g == 0) | (col_g == W)
    gram = exact_dot(vt[...], wt[...], ((1,), (1,)))
    gram = jnp.where(row_s > col_s, gram, 0.0)
    inv = unit_inverse(jnp.where(col_x, 0.0, gram), row_s, col_s, eye)
    f = exact_dot(inv, vt[...], ((1,), (0,)))
    m = exact_dot(inv, jnp.where(col_x, gram, 0.0), ((1,), (0,)))
    pad = jnp.zeros((S, B - N), F32)
    m_top = jnp.concatenate([m[0:S], pad], axis=1)
    m_low = jnp.concatenate([m[LAST:LAST + S], pad], axis=1)
    msg[0] = m_top
    msg[1] = m_low
    for i, there in ((0, up), (1, down)):
        copy = pltpu.make_async_remote_copy(
            src_ref=msg.at[i], dst_ref=near.at[i], send_sem=msg_sem.at[i], recv_sem=near_sem.at[i],
            device_id=(there, c), device_id_type=MESH)
        copy.start()
        sends.append(copy)

    f_hi, f_lo = split(f)
    f_both = jnp.concatenate([f_hi, f_lo], axis=0)
    for j in range(CHUNKS):
        at = pl.ds(j * width, width)
        both = jnp.dot(f_both, hi_ref[:, at], preferred_element_type=F32)
        p = both[:N] + both[N:] + jnp.dot(f_hi, lo_ref[:, at], preferred_element_type=F32)
        p_ref[:, at] = p
        hi, lo = split(p)
        c_ref[0:N, at] = hi
        c_ref[N:2 * N, at] = lo
        c_ref[2 * N:, at] = hi
        for i, there, first in ((0, up, 0), (1, down, LAST)):
            copy = pltpu.make_async_remote_copy(
                src_ref=p_ref.at[pl.ds(first, S), at], dst_ref=recv.at[i, :, at],
                send_sem=p_sem.at[i, j], recv_sem=recv_sem.at[i, j],
                device_id=(there, c), device_id_type=MESH)
            copy.start()
            sends.append(copy)

    for i, there in ((0, down), (1, up)):
        pltpu.make_async_remote_copy(
            src_ref=msg.at[i], dst_ref=near.at[i], send_sem=msg_sem.at[i], recv_sem=near_sem.at[i],
            device_id=(there, c), device_id_type=MESH).wait_recv()
    from_down = pltpu.roll(near[0], LAST, 1)
    from_up = pltpu.roll(near[1], B - LAST, 1)
    a_top = jnp.where(lane < S, m_top + jnp.where(r > 0, from_up, 0.0), 0.0) * tau_x[0]
    a_low = jnp.where((lane >= LAST) & (lane < LAST + S), m_low + jnp.where(r < R - 1, from_down, 0.0), 0.0) * tau_x[1]
    zero = jnp.zeros((S, B), F32)
    a = jnp.concatenate([a_top] + [zero] * (W - 1) + [a_low, zero], axis=0)[:, :N]
    tau_col = jnp.concatenate(
        [jnp.broadcast_to(tau_x[0], (S, N))] + [jnp.zeros((S, N), F32)] * (W - 1)
        + [jnp.broadcast_to(tau_x[1], (S, N)), jnp.zeros((S, N), F32)], axis=0)
    tau_row = jnp.sum(jnp.where(ri == ci, tau_col, 0.0), axis=0, keepdims=True)
    t = unit_inverse(a, row_s, col_s, eye) * tau_row
    inner = jnp.where(row_x, 0.0, m)
    left = jnp.where(row_x & (ri == ci), 1.0, 0.0) - inner
    k_t = jnp.where(col_x, exact_dot(left, t, ((1,), (0,))), eye)
    y = exact_dot(wt[...], k_t, ((0,), (0,)))
    y_hi, y_lo = split(y)
    y_ref[:, 0:N] = y_hi
    y_ref[:, N:2 * N] = y_hi
    y_ref[:, 2 * N:] = y_lo

    for j in range(CHUNKS):
        at = pl.ds(j * width, width)
        for i, there in ((0, down), (1, up)):
            pltpu.make_async_remote_copy(
                src_ref=p_ref.at[pl.ds(0, S), at], dst_ref=recv.at[i, :, at],
                send_sem=p_sem.at[i, j], recv_sem=recv_sem.at[i, j],
                device_id=(there, c), device_id_type=MESH).wait_recv()
        for first, i, keep in ((0, 1, r > 0), (LAST, 0, r < R - 1)):
            got = jnp.where(keep, recv[i, :, at], 0.0)
            x = jnp.concatenate([p_ref[first:first + S, at] + got, p_ref[first + S:first + 2 * S, at]], axis=0)
            hi, lo = split(x)
            c_ref[first:first + 2 * S, at] = hi
            c_ref[N + first:N + first + 2 * S, at] = lo
            c_ref[2 * N + first:2 * N + first + 2 * S, at] = hi
    for copy in sends:
        copy.wait_send()


def second_kernel(parts, e_ref, y_ref, c_ref, o_hbm, buf, sem):
    width = buf.shape[1] // parts

    def store(j):
        at = pl.ds(pl.multiple_of(j * width, width), width)
        return pltpu.make_async_copy(buf.at[:, at], o_hbm.at[:, at], sem.at[j])

    @pl.loop(0, parts)
    def _(j):
        at = pl.ds(pl.multiple_of(j * width, width), width)
        buf[:, at] = e_ref[:, at] - jnp.dot(y_ref[...], c_ref[:, at], preferred_element_type=F32)
        store(j).start()

    @pl.loop(0, parts)
    def _(j):
        store(j).wait()


def solution(mesh):
    R, C = mesh.shape["row"], mesh.shape["col"]

    def body(vectors_in, reflectors, offsets):
        rows, cols = vectors_in.shape
        chunks = 4 if cols % 2048 == 0 else 1
        vmem = pl.BlockSpec(memory_space=pltpu.VMEM)
        anywhere = pl.BlockSpec(memory_space=pl.ANY)
        dma = pltpu.SemaphoreType.DMA
        e, y, coeff = pl.pallas_call(
            functools.partial(first_kernel, R, C, chunks),
            out_shape=(
                pltpu.VMEM((rows, cols), F32),
                pltpu.VMEM((rows, 3 * N), BF16),
                pltpu.VMEM((3 * N, cols), BF16),
            ),
            in_specs=[pl.BlockSpec(memory_space=pltpu.SMEM), anywhere, anywhere],
            out_specs=(vmem, vmem, vmem),
            scratch_shapes=[
                pltpu.VMEM(reflectors.shape, F32),
                pltpu.VMEM((S, B), F32),
                pltpu.VMEM((2, C, S, B), F32),
                pltpu.VMEM((rows, cols), BF16),
                pltpu.VMEM((rows, cols), BF16),
                pltpu.VMEM((N, rows), F32),
                pltpu.VMEM((N, rows), F32),
                pltpu.VMEM((N, cols), F32),
                pltpu.VMEM((2, S, B), F32),
                pltpu.VMEM((2, S, B), F32),
                pltpu.VMEM((2, S, cols), F32),
                dma, dma((W,)), dma((2, C)), dma((2, C)), dma((2,)), dma((2,)), dma((2, chunks)), dma((2, chunks)),
            ],
            compiler_params=pltpu.CompilerParams(
                collective_id=0, has_side_effects=True, vmem_limit_bytes=24 * MIB
            ),
            name="reflect_one",
        )(
            offsets,
            pltpu.with_memory_space_constraint(vectors_in, pltpu.HBM),
            pltpu.with_memory_space_constraint(reflectors, pltpu.HBM),
        )
        parts = max(1, cols // 256)
        return pl.pallas_call(
            functools.partial(second_kernel, parts),
            out_shape=jax.ShapeDtypeStruct((rows, cols), F32),
            in_specs=[vmem, vmem, vmem],
            out_specs=anywhere,
            scratch_shapes=[pltpu.VMEM((rows, cols), F32), dma((parts,))],
            compiler_params=pltpu.CompilerParams(vmem_limit_bytes=16 * MIB),
            name="reflect_two",
        )(*(pltpu.with_memory_space_constraint(x, pltpu.VMEM) for x in (e, y, coeff)))

    in_specs = (P("row", "col"), P(None, "row", "col"), P())
    return jax.shard_map(body, mesh=mesh, in_specs=in_specs, out_specs=P("row", "col"), check_vma=False)
```

time: 779 us -> 26.6 us (0.03)
  the two profiles are of different devices: /device:TPU:25 before, /device:TPU:0 now
where the time goes in v1:
time: 26.6 us; the launch traced here: 26.5 us
  Pallas kernels  25.9 us (97%)
  local copies, waits for them, and re-layouts  0.65 us (2%)
    pallas_call x1, Pallas kernels, body(): pl.pallas_call(functools.partial(first_kernel, R, C, chunks), out_shape=(...  22.2 us
    pallas_call x1, Pallas kernels, body(): pl.pallas_call(functools.partial(second_kernel, parts), out_shape=jax.Sha...  3.67 us
    unnamed x2, local copies, waits for them, and re-layouts  0.65 us

profile of v1, /device:TPU:0, one launch (start us, length us, event | category | flops | bytes accessed | tf_op | source)
XLA Modules:
  0.0 26.5 jit_solution(3754962653391306740)
XLA Ops:
  0.0 0.0 copy-start
  0.0 0.7 %copy-done = s32[8]{0:T(128)S(1)} copy-done((s32[8]{0:T(128)S(1)}, s32[8]{0:T(128)}, u32[]{:S(2)}) %copy-start) | copy-done | bytes 56
  0.7 22.2 %reflect_one.1 = (f32[1024,2048]{1,0:T(8,128)S(1)}, bf16[1024,240]{1,0:T(8,128)(2,1)S(1)}, bf16[240,2048]{1,0:T(8,128)(2,1)S(1)}) custom-call(s32[8]{0:T(128)S(1)} %copy-done, f32[1024,2048]{1,0:T(8,128)} %e_hbm.1, f32[8,8,16]{2,1,0:T(8,128)} %refl_hbm.1), custom_call_target="tpu_custom_call" | custom-call | tf_op jit(solution)/shard_map/reflect_one/pallas_call | solution.py:274
  22.9 3.7 %reflect_two.1 = f32[1024,2048]{1,0:T(8,128)} custom-call(f32[1024,2048]{1,0:T(8,128)S(1)} %get-tuple-element.8.e_ref, bf16[1024,240]{1,0:T(8,128)(2,1)S(1)} %get-tuple-element.9.y_ref, bf16[240,2048]{1,0:T(8,128)(2,1)S(1)} %get-tuple-element.10.c_ref), custom_call_target="tpu_custom_call" | custom-call | tf_op jit(solution)/shard_map/reflect_two/pallas_call | solution.py:307
Async XLA Ops:
  0.0 0.7 %copy-start = (s32[8]{0:T(128)S(1)}, s32[8]{0:T(128)}, u32[]{:S(2)}) copy-start(s32[8]{0:T(128)} %off_ref.1) | copy-start | bytes 100

commit v2 on v0

v2 whole, which is shorter than its diff:
```python
import functools

import jax
import jax.numpy as jnp
from jax import lax
from jax.experimental import pallas as pl
from jax.experimental.pallas import tpu as pltpu
from jax.sharding import PartitionSpec as P

MESH = pl.DeviceIdType.MESH
F32 = jnp.float32
BF16 = jnp.bfloat16
EPS = 1e-6
S = 8
W = 8
B = 128
I = S * W
N = I + 2 * S
MIB = 1 << 20


def split(x):
    hi = x.astype(BF16)
    return hi, (x - hi.astype(F32)).astype(BF16)


def wide(x, width):
    return jnp.concatenate([x] * (width // B), axis=1) if width > B else x


def row_of(x, i):
    return jnp.broadcast_to(x[i:i + 1], x.shape)


def gather_rows(tiles, i):
    sub = lax.broadcasted_iota(jnp.int32, tiles[0].shape, 0)
    out = jnp.zeros_like(tiles[0])
    for s, tile in enumerate(tiles):
        out = jnp.where(sub == s, row_of(tile, i), out)
    return out


def lane_sum(x):
    return jnp.broadcast_to(jnp.sum(x, axis=1, keepdims=True), x.shape)


def solve(u, own, after, before, tau, width):
    p, c, nexts, prevs = [], [], [], []
    for s in range(S):
        acc = u[s]
        for t in range(s):
            acc = acc - wide(own(s, t), width) * c[t]
            acc = acc - wide(after(s, t), width) * nexts[t]
            acc = acc - wide(before(s, t), width) * prevs[t]
        p.append(acc)
        c.append(acc * wide(tau(s), width))
        nexts.append(pltpu.roll(c[s], W - 1, 0))
        prevs.append(pltpu.roll(c[s], 1, 0))
    return p, c


def first_kernel(
    R, C, CHUNKS,
    off_hbm, e_hbm, refl_hbm,
    e_ref, y_ref, c_ref,
    off_ref, refl, mine, gat, hi_ref, lo_ref, vt, coef, fact, edge, top, low_ref, top_ref, msg, near, recv,
    off_sem, refl_sem, e_sem, out_sem, gat_sem, edge_sem, top_sem, msg_sem, near_sem, p_sem, recv_sem,
):
    r = lax.axis_index("row")
    c = lax.axis_index("col")
    up = lax.max(r - 1, 0)
    down = lax.min(r + 1, R - 1)
    has_up, has_down = r > 0, r < R - 1
    rows, cols = e_ref.shape
    step = rows // W
    width = cols // CHUNKS
    piece = refl.shape[2]

    barrier = pltpu.get_barrier_semaphore()
    for d in range(1, C):
        pl.semaphore_signal(barrier, inc=1, device_id=(r, lax.rem(c + d, C)), device_id_type=MESH)

    @pl.when(has_up)
    def _():
        pl.semaphore_signal(barrier, inc=1, device_id=(up, c), device_id_type=MESH)

    @pl.when(has_down)
    def _():
        pl.semaphore_signal(barrier, inc=1, device_id=(down, c), device_id_type=MESH)

    refl_copy = pltpu.make_async_copy(refl_hbm, refl, refl_sem)
    refl_copy.start()
    off_copy = pltpu.make_async_copy(off_hbm, off_ref, off_sem)
    off_copy.start()
    loads = []
    for i in range(W):
        part = pl.ds(i * step, step)
        load = pltpu.make_async_copy(e_hbm.at[part], e_ref.at[part], e_sem.at[i])
        load.start()
        loads.append(load)

    refl_copy.wait()
    tile = jnp.concatenate([refl[s] for s in range(S)], axis=1)
    mine[...] = tile
    pl.semaphore_wait(barrier, C - 1 + lax.min(r, 1) + lax.min(R - 1 - r, 1))

    sends = []
    for d in range(1, C):
        sends.append(pltpu.make_async_remote_copy(
            src_ref=mine, dst_ref=gat.at[c], send_sem=out_sem.at[d], recv_sem=gat_sem.at[c],
            device_id=(r, lax.rem(c + d, C)), device_id_type=MESH))
    for copy in sends:
        copy.start()
    gat[c] = tile

    def edge_copy(to):
        return pltpu.make_async_remote_copy(
            src_ref=edge, dst_ref=top, send_sem=edge_sem, recv_sem=top_sem,
            device_id=(to, c), device_id_type=MESH)

    def msg_copy(i, to):
        return pltpu.make_async_remote_copy(
            src_ref=msg.at[i], dst_ref=near.at[i], send_sem=msg_sem.at[i], recv_sem=near_sem.at[i],
            device_id=(to, c), device_id_type=MESH)

    def sum_copy(i, j, to):
        at = pl.ds(j * width, width)
        return pltpu.make_async_remote_copy(
            src_ref=(top_ref, low_ref)[i].at[:, at], dst_ref=recv.at[i, :, at],
            send_sem=p_sem.at[i, j], recv_sem=recv_sem.at[i, j],
            device_id=(to, c), device_id_type=MESH)

    @pl.when(r == 0)
    def _():
        top[...] = jnp.zeros_like(top)
        near[1] = jnp.zeros((S, B), F32)
        recv[1] = jnp.zeros((S, cols), F32)

    @pl.when(r == R - 1)
    def _():
        near[0] = jnp.zeros((S, B), F32)
        recv[0] = jnp.zeros((S, cols), F32)

    vt[...] = jnp.zeros_like(vt)

    for i in range(W):
        loads[i].wait()

        @pl.loop(0, cols // 512)
        def _(j):
            at = (pl.ds(i * step, step), pl.ds(pl.multiple_of(j * 512, 512), 512))
            hi, lo = split(e_ref[at])
            hi_ref[at] = hi
            lo_ref[at] = lo

    off_copy.wait()
    lane = lax.broadcasted_iota(jnp.int32, (S, B), 1)
    sub = lax.broadcasted_iota(jnp.int32, (S, B), 0)

    for d in range(1, C):
        src = lax.rem(c + d, C)
        pltpu.make_async_remote_copy(
            src_ref=mine, dst_ref=gat.at[src], send_sem=out_sem.at[d], recv_sem=gat_sem.at[src],
            device_id=(r, src), device_id_type=MESH).wait_recv()

    parts = [gat[q] for q in range(C)]
    turned, heres, overs, taus = [], [], [], []
    for s in range(S):
        x = jnp.zeros((W, B), F32)
        for q in range(C):
            turn = ((q - s) * piece) % B
            y = parts[q] if turn == 0 else pltpu.roll(parts[q], turn, 1)
            x = jnp.where((lane >= q * piece) & (lane < (q + 1) * piece), y, x)
        o = off_ref[s]
        for b in range(7):
            x = jnp.where(((o >> b) & 1) == 1, pltpu.roll(x, 1 << b, 1), x)
        turned.append(x)
    edge[...] = gather_rows(turned, W - 1)

    @pl.when(has_down)
    def _():
        edge_copy(down).start()

    for s in range(S):
        x, o = turned[s], off_ref[s]
        here = jnp.where(lane >= o, x, 0.0)
        over = jnp.where(lane < o, x, 0.0)
        whole = here * here + jnp.where((sub < W - 1) | has_down, over * over, 0.0)
        taus.append(2.0 / (lane_sum(whole) + EPS))
        over = jnp.where(sub < W - 1, over, 0.0)
        heres.append(here)
        overs.append(over)
        fact[s] = jnp.where(sub < W - 1, taus[s], 0.0)
    tau_low = gather_rows(taus, W - 1)
    for q in range(S // 2):
        for t in range(W):
            pair = []
            for s in (2 * q, 2 * q + 1):
                x = jnp.where(sub == t, heres[s], 0.0)
                if t > 0:
                    x = x + jnp.where(sub == t - 1, overs[s], 0.0)
                pair.append(x)
            hi, lo = split(jnp.concatenate(pair, axis=0))
            at = pl.ds(t * B, B)
            vt[q * 2 * W:(q + 1) * 2 * W, at] = hi
            vt[N + q * 2 * W:N + (q + 1) * 2 * W, at] = lo
            vt[2 * N + q * 2 * W:2 * N + (q + 1) * 2 * W, at] = hi

    def pair_index(s, t):
        return s * (s - 1) // 2 + t

    for s in range(S):
        for t in range(s):
            own = lane_sum(heres[s] * heres[t] + overs[s] * overs[t])
            after = lane_sum(overs[s] * pltpu.roll(heres[t], W - 1, 0))
            before = lane_sum(heres[s] * pltpu.roll(overs[t], 1, 0))
            n = pair_index(s, t)
            coef[0, n] = own
            coef[1, n] = after
            coef[2, n] = before

    def solved(u, w):
        return solve(
            u, lambda s, t: coef[0, pair_index(s, t)], lambda s, t: coef[1, pair_index(s, t)],
            lambda s, t: coef[2, pair_index(s, t)], lambda s: fact[s], w)

    first_rows = []
    for j in range(CHUNKS):
        at = pl.ds(j * width, width)
        both = jnp.dot(vt[0:2 * N, :], hi_ref[:, at], preferred_element_type=F32)
        u = both[:I] + both[N:N + I] + jnp.dot(vt[0:I, :], lo_ref[:, at], preferred_element_type=F32)
        p, cs = solved([u[s * W:(s + 1) * W] for s in range(S)], width)
        low_ref[:, at] = gather_rows(p, W - 1)

        @pl.when(has_down)
        def _():
            sum_copy(1, j, down).start()

        first_rows.append([x[0:1] for x in cs])
        for q in range(S // 2):
            hi, lo = split(jnp.concatenate(cs[2 * q:2 * q + 2], axis=0))
            c_ref[q * 2 * W:(q + 1) * 2 * W, at] = hi
            c_ref[N + q * 2 * W:N + (q + 1) * 2 * W, at] = lo
            c_ref[2 * N + q * 2 * W:2 * N + (q + 1) * 2 * W, at] = hi

    @pl.when(has_up)
    def _():
        edge_copy(up).wait_recv()

    off = jnp.zeros((S, B), jnp.int32)
    for s in range(S):
        off = jnp.where(sub == s, off_ref[s], off)
    x = top[...]
    tau_top = jnp.where(has_up, 2.0 / (lane_sum(x * x) + EPS), 0.0)
    x = jnp.where(lane < off, x, 0.0)
    hi, lo = split(jnp.concatenate([jnp.zeros((S, B), F32), x], axis=0))
    vt[I:N, 0:B] = hi
    vt[N + I:2 * N, 0:B] = lo
    vt[2 * N + I:3 * N, 0:B] = hi
    first = gather_rows(heres, 0)
    into = [jnp.where(sub > s, lane_sum(x * row_of(heres[s], 0)), 0.0) for s in range(S)]
    meet = jnp.zeros((S, B), F32)
    tops = jnp.zeros((S, B), F32)
    for t in range(S):
        mark = (lane == I + S + t) & (sub > t)
        meet = jnp.where(mark, lane_sum(first * row_of(x, t)), meet)
        tops = jnp.where(mark, lane_sum(x * row_of(x, t)), tops)
    answer = []
    for s in range(S):
        y = jnp.where(sub == 0, row_of(meet, s), 0.0)
        for t in range(s):
            n = pair_index(s, t)
            y = jnp.where(lane == I + t, jnp.where(sub == W - 1, coef[0, n], jnp.where(sub == W - 2, coef[1, n], 0.0)), y)
        answer.append(y)
    p_m, c_m = solved(answer, B)
    a_low = gather_rows(p_m, W - 1)
    a_top = tops
    for s in range(S):
        a_top = a_top - into[s] * row_of(c_m[s], 0)
    msg[0] = a_top
    msg[1] = a_low

    v_top = jnp.concatenate([hi, lo], axis=0)

    for i, has, there in ((0, has_up, up), (1, has_down, down)):
        @pl.when(has)
        def _():
            msg_copy(i, there).start()

    for j in range(CHUNKS):
        at = pl.ds(j * width, width)
        both = jnp.dot(v_top, hi_ref[0:B, at], preferred_element_type=F32)
        acc = both[S:2 * S] + both[3 * S:] + jnp.dot(hi, lo_ref[0:B, at], preferred_element_type=F32)[S:]
        for s in range(S):
            acc = acc - wide(into[s], width) * jnp.broadcast_to(first_rows[j][s], (S, width))
        top_ref[:, at] = acc

        @pl.when(has_up)
        def _():
            sum_copy(0, j, up).start()

    k_t = []
    for s in range(S):
        x = jnp.where((lane == s * W + sub) & (sub < W - 1), 1.0, 0.0) - c_m[s]
        k_t.append(x + jnp.where((sub == W - 1) & (lane == I + s), 1.0, 0.0))
    k_t.append(jnp.zeros((S, B), F32))
    k_t.append(jnp.where(lane == I + S + sub, 1.0, 0.0))
    k_t = jnp.concatenate(k_t, axis=0)[:, :N]
    k_t = jnp.concatenate([k_t, k_t, k_t], axis=1)
    hi, lo = split(k_t)
    k_t = jnp.concatenate([hi, hi, lo], axis=0)
    y = lax.dot_general(vt[...], k_t, (((0,), (0,)), ((), ())), preferred_element_type=F32)
    hi, lo = split(y)
    spot = lax.broadcasted_iota(jnp.int32, y.shape, 1)
    y_ref[...] = jnp.where(spot < 2 * N, hi, lo)

    @pl.when(has_down)
    def _():
        msg_copy(0, down).wait_recv()

    @pl.when(has_up)
    def _():
        msg_copy(1, up).wait_recv()

    a_low = a_low + pltpu.roll(near[0], B - S, 1)
    a_top = a_top + pltpu.roll(near[1], S, 1)
    low_cols = [jnp.broadcast_to(a_low[:, I + t:I + t + 1], (S, B)) for t in range(S)]
    top_cols = [jnp.broadcast_to(a_top[:, I + S + t:I + S + t + 1], (S, B)) for t in range(S)]
    for j in range(CHUNKS):
        at = pl.ds(j * width, width)

        @pl.when(has_down)
        def _():
            sum_copy(0, j, down).wait_recv()

        @pl.when(has_up)
        def _():
            sum_copy(1, j, up).wait_recv()

        both = []
        for ref, i, tau, a in ((low_ref, 0, tau_low, low_cols), (top_ref, 1, tau_top, top_cols)):
            acc = ref[:, at] + recv[i, :, at]
            for t in range(S - 1):
                acc = acc - wide(a[t], width) * row_of(acc * wide(tau, width), t)
            both.append(acc * wide(tau, width))
        hi, lo = split(jnp.concatenate(both, axis=0))
        c_ref[I:N, at] = hi
        c_ref[N + I:2 * N, at] = lo
        c_ref[2 * N + I:3 * N, at] = hi

    for copy in sends:
        copy.wait_send()

    @pl.when(has_up)
    def _():
        msg_copy(0, up).wait_send()
        for j in range(CHUNKS):
            sum_copy(0, j, up).wait_send()

    @pl.when(has_down)
    def _():
        edge_copy(down).wait_send()
        msg_copy(1, down).wait_send()
        for j in range(CHUNKS):
            sum_copy(1, j, down).wait_send()


def second_kernel(parts, e_ref, y_ref, c_ref, o_hbm, buf, sem):
    width = buf.shape[1] // parts

    def store(j):
        at = pl.ds(pl.multiple_of(j * width, width), width)
        return pltpu.make_async_copy(buf.at[:, at], o_hbm.at[:, at], sem.at[j])

    @pl.loop(0, parts)
    def _(j):
        at = pl.ds(pl.multiple_of(j * width, width), width)
        buf[:, at] = e_ref[:, at] - jnp.dot(y_ref[...], c_ref[:, at], preferred_element_type=F32)
        store(j).start()

    @pl.loop(0, parts)
    def _(j):
        store(j).wait()


def solution(mesh):
    R, C = mesh.shape["row"], mesh.shape["col"]

    def body(vectors_in, reflectors, offsets):
        rows, cols = vectors_in.shape
        chunks = 4 if cols % 2048 == 0 else 1
        vmem = pl.BlockSpec(memory_space=pltpu.VMEM)
        anywhere = pl.BlockSpec(memory_space=pl.ANY)
        dma = pltpu.SemaphoreType.DMA
        e, y, coeff = pl.pallas_call(
            functools.partial(first_kernel, R, C, chunks),
            out_shape=(
                pltpu.VMEM((rows, cols), F32),
                pltpu.VMEM((rows, 3 * N), BF16),
                pltpu.VMEM((3 * N, cols), BF16),
            ),
            in_specs=[anywhere] * 3,
            out_specs=(vmem, vmem, vmem),
            scratch_shapes=[
                pltpu.SMEM((S,), jnp.int32),
                pltpu.VMEM(reflectors.shape, F32),
                pltpu.VMEM((W, B), F32),
                pltpu.VMEM((C, W, B), F32),
                pltpu.VMEM((rows, cols), BF16),
                pltpu.VMEM((rows, cols), BF16),
                pltpu.VMEM((3 * N, rows), BF16),
                pltpu.VMEM((3, S * (S - 1) // 2, W, B), F32),
                pltpu.VMEM((S, W, B), F32),
                pltpu.VMEM((S, B), F32),
                pltpu.VMEM((S, B), F32),
                pltpu.VMEM((S, cols), F32),
                pltpu.VMEM((S, cols), F32),
                pltpu.VMEM((2, S, B), F32),
                pltpu.VMEM((2, S, B), F32),
                pltpu.VMEM((2, S, cols), F32),
                dma, dma, dma((W,)), dma((C,)), dma((C,)), dma, dma,
                dma((2,)), dma((2,)), dma((2, chunks)), dma((2, chunks)),
            ],
            compiler_params=pltpu.CompilerParams(
                collective_id=0, has_side_effects=True, vmem_limit_bytes=24 * MIB
            ),
            name="reflect_one",
        )(
            pltpu.with_memory_space_constraint(offsets, pltpu.HBM),
            pltpu.with_memory_space_constraint(vectors_in, pltpu.HBM),
            pltpu.with_memory_space_constraint(reflectors, pltpu.HBM),
        )
        parts = max(1, cols // 256)
        return pl.pallas_call(
            functools.partial(second_kernel, parts),
            out_shape=jax.ShapeDtypeStruct((rows, cols), F32),
            in_specs=[vmem, vmem, vmem],
            out_specs=anywhere,
            scratch_shapes=[pltpu.VMEM((rows, cols), F32), dma((parts,))],
            compiler_params=pltpu.CompilerParams(vmem_limit_bytes=16 * MIB),
            name="reflect_two",
        )(*(pltpu.with_memory_space_constraint(x, pltpu.VMEM) for x in (e, y, coeff)))

    in_specs = (P("row", "col"), P(None, "row", "col"), P())
    return jax.shard_map(body, mesh=mesh, in_specs=in_specs, out_specs=P("row", "col"), check_vma=False)
```

time: 779 us -> 22.2 us (0.03); the launches traced: 763 us -> 22.1 us
  local copies, waits for them, and re-layouts: 255 us -> 0 us
  blocking collectives: 177 us -> 0 us
  starting transfers between devices: 130 us -> 0 us
  other arithmetic: 107 us -> 0 us
  waiting for transfers between devices: 40.6 us -> 0 us
  matrix products: 32.3 us -> 0 us
  Pallas kernels: 0 us -> 22.1 us
  between operations: 20.7 us -> 0.01 us
    all_gather x8 -> x0, blocking collectives: 177 us -> none  [body(): vecs = lax.all_gather(reflectors[sweep], 'col', axis=1, tiled=True)]
    dynamic_update_slice x8 -> x0, local copies, waits for them, and re-layouts: 174 us -> none  [body(): extended = lax.dynamic_update_slice_in_dim(extended, window, start, 0)]
    ppermute x16 -> x0, starting transfers between devices: 130 us -> none  [passed_along(): return lax.ppermute(block, axis, route)]
    sub x8 -> x0, other arithmetic: 61.2 us -> none  [reflect(): tiles - vecs[:, :, None] * coeff[:, None, :]]
    slice x19 -> x0, local copies, waits for them, and re-layouts: 42.9 us -> none  [the longest x8 30.2 us: body(): matrix = jnp.concatenate([leading, extended[half:local_rows]], axis=0)]
    ppermute x16 -> x0, waiting for transfers between devices: 40.6 us -> none  [passed_along(): return lax.ppermute(block, axis, route)]
    dynamic_slice x8 -> x0, local copies, waits for them, and re-layouts: 32.6 us -> none  [body(): window = lax.dynamic_slice_in_dim(extended, start, local_rows, 0)]
    dot_general x8 -> x0, matrix products: 32.3 us -> none  [reflect(): jnp.einsum('kb,kbc->kc', vecs, tiles, precision=lax.Precision.HIGHEST)]
  transfers between devices with their start and end apart: 16 -> 0, of which waited for: 8 -> 0; matrix products, arithmetic and copies ran while one was open for 6% -> 0% of each run, Pallas kernels for 0% -> 0%
where the time goes in v2:
time: 22.2 us; the launch traced here: 22.1 us
  Pallas kernels  22.1 us (100%)
    pallas_call x1, Pallas kernels, body(): pl.pallas_call(functools.partial(first_kernel, R, C, chunks), out_shape=(...  18.4 us
    pallas_call x1, Pallas kernels, body(): pl.pallas_call(functools.partial(second_kernel, parts), out_shape=jax.Sha...  3.66 us

profile of v2, /device:TPU:25, one launch (start us, length us, event | category | flops | bytes accessed | tf_op | source)
XLA Modules:
  0.0 22.1 jit_solution(13434400526121161627)
XLA Ops:
  0.0 18.4 %reflect_one.1 = (f32[1024,2048]{1,0:T(8,128)S(1)}, bf16[1024,240]{1,0:T(8,128)(2,1)S(1)}, bf16[240,2048]{1,0:T(8,128)(2,1)S(1)}) custom-call(s32[8]{0:T(128)} %off_hbm.1, f32[1024,2048]{1,0:T(8,128)} %e_hbm.1, f32[8,8,16]{2,1,0:T(8,128)} %refl_hbm.1), custom_call_target="tpu_custom_call" | custom-call | tf_op jit(solution)/shard_map/reflect_one/pallas_call | solution.py:395
  18.4 3.7 %reflect_two.1 = f32[1024,2048]{1,0:T(8,128)} custom-call(f32[1024,2048]{1,0:T(8,128)S(1)} %get-tuple-element.8.e_ref, bf16[1024,240]{1,0:T(8,128)(2,1)S(1)} %get-tuple-element.9.y_ref, bf16[240,2048]{1,0:T(8,128)(2,1)S(1)} %get-tuple-element.10.c_ref), custom_call_target="tpu_custom_call" | custom-call | tf_op jit(solution)/shard_map/reflect_two/pallas_call | solution.py:434

commit v3 on v2

--- a/solution.py
+++ b/solution.py
@@ -16,6 +16,7 @@
 B = 128
 I = S * W
 N = I + 2 * S
+EARLY = 3
 MIB = 1 << 20
 
 
@@ -74,6 +75,7 @@
     rows, cols = e_ref.shape
     step = rows // W
     width = cols // CHUNKS
+    TOP = CHUNKS - 1
     piece = refl.shape[2]
 
     barrier = pltpu.get_barrier_semaphore()
@@ -95,9 +97,9 @@
     loads = []
     for i in range(W):
         part = pl.ds(i * step, step)
-        load = pltpu.make_async_copy(e_hbm.at[part], e_ref.at[part], e_sem.at[i])
+        loads.append(pltpu.make_async_copy(e_hbm.at[part], e_ref.at[part], e_sem.at[i]))
+    for load in loads[:EARLY]:
         load.start()
-        loads.append(load)
 
     refl_copy.wait()
     tile = jnp.concatenate([refl[s] for s in range(S)], axis=1)
@@ -105,12 +107,14 @@
     pl.semaphore_wait(barrier, C - 1 + lax.min(r, 1) + lax.min(R - 1 - r, 1))
 
     sends = []
-    for d in range(1, C):
+    for d in sorted(range(1, C), key=lambda d: abs(d - C // 2)):
         sends.append(pltpu.make_async_remote_copy(
             src_ref=mine, dst_ref=gat.at[c], send_sem=out_sem.at[d], recv_sem=gat_sem.at[c],
             device_id=(r, lax.rem(c + d, C)), device_id_type=MESH))
     for copy in sends:
         copy.start()
+    for load in loads[EARLY:]:
+        load.start()
     gat[c] = tile
 
     def edge_copy(to):
@@ -143,15 +147,13 @@
 
     vt[...] = jnp.zeros_like(vt)
 
-    for i in range(W):
-        loads[i].wait()
-
-        @pl.loop(0, cols // 512)
-        def _(j):
-            at = (pl.ds(i * step, step), pl.ds(pl.multiple_of(j * 512, 512), 512))
-            hi, lo = split(e_ref[at])
-            hi_ref[at] = hi
-            lo_ref[at] = lo
+    @pl.loop(0, W)
+    def _(i):
+        part = pl.ds(pl.multiple_of(i * step, step), step)
+        pltpu.make_async_copy(e_hbm.at[part], e_ref.at[part], e_sem.at[i]).wait()
+        hi, lo = split(e_ref[part])
+        hi_ref[part] = hi
+        lo_ref[part] = lo
 
     off_copy.wait()
     lane = lax.broadcasted_iota(jnp.int32, (S, B), 1)
@@ -172,9 +174,7 @@
             y = parts[q] if turn == 0 else pltpu.roll(parts[q], turn, 1)
             x = jnp.where((lane >= q * piece) & (lane < (q + 1) * piece), y, x)
         o = off_ref[s]
-        for b in range(7):
-            x = jnp.where(((o >> b) & 1) == 1, pltpu.roll(x, 1 << b, 1), x)
-        turned.append(x)
+        turned.append(pltpu.roll(x, o, 1))
     edge[...] = gather_rows(turned, W - 1)
 
     @pl.when(has_down)
@@ -224,6 +224,64 @@
             u, lambda s, t: coef[0, pair_index(s, t)], lambda s, t: coef[1, pair_index(s, t)],
             lambda s, t: coef[2, pair_index(s, t)], lambda s: fact[s], w)
 
+    def top_part():
+        @pl.when(has_up)
+        def _():
+            edge_copy(up).wait_recv()
+
+        off = jnp.zeros((S, B), jnp.int32)
+        for s in range(S):
+            off = jnp.where(sub == s, off_ref[s], off)
+        x = top[...]
+        tau_top = jnp.where(has_up, 2.0 / (lane_sum(x * x) + EPS), 0.0)
+        x = jnp.where(lane < off, x, 0.0)
+        hi, lo = split(jnp.concatenate([jnp.zeros((S, B), F32), x], axis=0))
+        vt[I:N, 0:B] = hi
+        vt[N + I:2 * N, 0:B] = lo
+        vt[2 * N + I:3 * N, 0:B] = hi
+        first = gather_rows(heres, 0)
+        into = [jnp.where(sub > s, lane_sum(x * row_of(heres[s], 0)), 0.0) for s in range(S)]
+        meet = jnp.zeros((S, B), F32)
+        tops = jnp.zeros((S, B), F32)
+        for t in range(S):
+            mark = (lane == I + S + t) & (sub > t)
+            meet = jnp.where(mark, lane_sum(first * row_of(x, t)), meet)
+            tops = jnp.where(mark, lane_sum(x * row_of(x, t)), tops)
+        answer = []
+        for s in range(S):
+            y = jnp.where(sub == 0, row_of(meet, s), 0.0)
+            for t in range(s):
+                n = pair_index(s, t)
+                y = jnp.where(lane == I + t, jnp.where(sub == W - 1, coef[0, n], jnp.where(sub == W - 2, coef[1, n], 0.0)), y)
+            answer.append(y)
+        p_m, c_m = solved(answer, B)
+        a_low = gather_rows(p_m, W - 1)
+        a_top = tops
+        for s in range(S):
+            a_top = a_top - into[s] * row_of(c_m[s], 0)
+        msg[0] = a_top
+        msg[1] = a_low
+
+        v_top = jnp.concatenate([hi, lo], axis=0)
+
+        for i, has, there in ((0, has_up, up), (1, has_down, down)):
+            @pl.when(has)
+            def _():
+                msg_copy(i, there).start()
+        return v_top, into, tau_top, a_top, a_low, c_m
+
+    def top_sums(j):
+        at = pl.ds(j * width, width)
+        both = jnp.dot(v_top, hi_ref[0:B, at], preferred_element_type=F32)
+        acc = both[S:2 * S] + both[3 * S:] + jnp.dot(v_top[:2 * S], lo_ref[0:B, at], preferred_element_type=F32)[S:]
+        for s in range(S):
+            acc = acc - wide(into[s], width) * jnp.broadcast_to(first_rows[j][s], (S, width))
+        top_ref[:, at] = acc
+
+        @pl.when(has_up)
+        def _():
+            sum_copy(0, j, up).start()
+
     first_rows = []
     for j in range(CHUNKS):
         at = pl.ds(j * width, width)
@@ -243,61 +301,12 @@
             c_ref[N + q * 2 * W:N + (q + 1) * 2 * W, at] = lo
             c_ref[2 * N + q * 2 * W:2 * N + (q + 1) * 2 * W, at] = hi
 
-    @pl.when(has_up)
-    def _():
-        edge_copy(up).wait_recv()
-
-    off = jnp.zeros((S, B), jnp.int32)
-    for s in range(S):
-        off = jnp.where(sub == s, off_ref[s], off)
-    x = top[...]
-    tau_top = jnp.where(has_up, 2.0 / (lane_sum(x * x) + EPS), 0.0)
-    x = jnp.where(lane < off, x, 0.0)
-    hi, lo = split(jnp.concatenate([jnp.zeros((S, B), F32), x], axis=0))
-    vt[I:N, 0:B] = hi
-    vt[N + I:2 * N, 0:B] = lo
-    vt[2 * N + I:3 * N, 0:B] = hi
-    first = gather_rows(heres, 0)
-    into = [jnp.where(sub > s, lane_sum(x * row_of(heres[s], 0)), 0.0) for s in range(S)]
-    meet = jnp.zeros((S, B), F32)
-    tops = jnp.zeros((S, B), F32)
-    for t in range(S):
-        mark = (lane == I + S + t) & (sub > t)
-        meet = jnp.where(mark, lane_sum(first * row_of(x, t)), meet)
-        tops = jnp.where(mark, lane_sum(x * row_of(x, t)), tops)
-    answer = []
-    for s in range(S):
-        y = jnp.where(sub == 0, row_of(meet, s), 0.0)
-        for t in range(s):
-            n = pair_index(s, t)
-            y = jnp.where(lane == I + t, jnp.where(sub == W - 1, coef[0, n], jnp.where(sub == W - 2, coef[1, n], 0.0)), y)
-        answer.append(y)
-    p_m, c_m = solved(answer, B)
-    a_low = gather_rows(p_m, W - 1)
-    a_top = tops
-    for s in range(S):
-        a_top = a_top - into[s] * row_of(c_m[s], 0)
-    msg[0] = a_top
-    msg[1] = a_low
-
-    v_top = jnp.concatenate([hi, lo], axis=0)
-
-    for i, has, there in ((0, has_up, up), (1, has_down, down)):
-        @pl.when(has)
-        def _():
-            msg_copy(i, there).start()
-
-    for j in range(CHUNKS):
-        at = pl.ds(j * width, width)
-        both = jnp.dot(v_top, hi_ref[0:B, at], preferred_element_type=F32)
-        acc = both[S:2 * S] + both[3 * S:] + jnp.dot(hi, lo_ref[0:B, at], preferred_element_type=F32)[S:]
-        for s in range(S):
-            acc = acc - wide(into[s], width) * jnp.broadcast_to(first_rows[j][s], (S, width))
-        top_ref[:, at] = acc
-
-        @pl.when(has_up)
-        def _():
-            sum_copy(0, j, up).start()
+        if j == TOP:
+            v_top, into, tau_top, a_top, a_low, c_m = top_part()
+            for i in range(j):
+                top_sums(i)
+        if j >= TOP:
+            top_sums(j)
 
     k_t = []
     for s in range(S):

time: 22.2 us -> 21.4 us (0.964)
  Pallas kernels: 22.1 us -> 21.3 us
    pallas_call x1, Pallas kernels: 18.4 us -> 17.7 us  [body(): pl.pallas_call(functools.partial(first_kernel, R, C, chunks), out_shape=(...]
where the time goes in v3:
time: 21.4 us; the launch traced here: 21.3 us
  Pallas kernels  21.3 us (100%)
    pallas_call x1, Pallas kernels, body(): pl.pallas_call(functools.partial(first_kernel, R, C, chunks), out_shape=(...  17.7 us
    pallas_call x1, Pallas kernels, body(): pl.pallas_call(functools.partial(second_kernel, parts), out_shape=jax.Sha...  3.67 us

profile of v3, /device:TPU:25, one launch (start us, length us, event | category | flops | bytes accessed | tf_op | source)
XLA Modules:
  0.0 21.3 jit_solution(11801588794547943714)
XLA Ops:
  0.0 17.7 %reflect_one.1 = (f32[1024,2048]{1,0:T(8,128)S(1)}, bf16[1024,240]{1,0:T(8,128)(2,1)S(1)}, bf16[240,2048]{1,0:T(8,128)(2,1)S(1)}) custom-call(s32[8]{0:T(128)} %off_hbm.1, f32[1024,2048]{1,0:T(8,128)} %e_hbm.1, f32[8,8,16]{2,1,0:T(8,128)} %refl_hbm.1), custom_call_target="tpu_custom_call" | custom-call | tf_op jit(solution)/shard_map/reflect_one/pallas_call | solution.py:404
  17.7 3.7 %reflect_two.1 = f32[1024,2048]{1,0:T(8,128)} custom-call(f32[1024,2048]{1,0:T(8,128)S(1)} %get-tuple-element.8.e_ref, bf16[1024,240]{1,0:T(8,128)(2,1)S(1)} %get-tuple-element.9.y_ref, bf16[240,2048]{1,0:T(8,128)(2,1)S(1)} %get-tuple-element.10.c_ref), custom_call_target="tpu_custom_call" | custom-call | tf_op jit(solution)/shard_map/reflect_two/pallas_call | solution.py:443

commit v4 on v3

--- a/solution.py
+++ b/solution.py
@@ -166,13 +166,21 @@
             device_id=(r, src), device_id_type=MESH).wait_recv()
 
     parts = [gat[q] for q in range(C)]
+    blocks = [(lane >= q * piece) & (lane < (q + 1) * piece) for q in range(C)]
+
+    def pick(tiles):
+        out = tiles[0]
+        for q in range(1, C):
+            out = jnp.where(blocks[q], tiles[q], out)
+        return out
+
+    moved = []
+    for d in range(C):
+        y = pick([parts[(s + d) % C] for s in range(S)])
+        moved.append(y if d == 0 else pltpu.roll(y, d * piece, 1))
     turned, heres, overs, taus = [], [], [], []
     for s in range(S):
-        x = jnp.zeros((W, B), F32)
-        for q in range(C):
-            turn = ((q - s) * piece) % B
-            y = parts[q] if turn == 0 else pltpu.roll(parts[q], turn, 1)
-            x = jnp.where((lane >= q * piece) & (lane < (q + 1) * piece), y, x)
+        x = pick([moved[(q - s) % C] for q in range(C)])
         o = off_ref[s]
         turned.append(pltpu.roll(x, o, 1))
     edge[...] = gather_rows(turned, W - 1)
@@ -397,7 +405,7 @@
 
     def body(vectors_in, reflectors, offsets):
         rows, cols = vectors_in.shape
-        chunks = 4 if cols % 2048 == 0 else 1
+        chunks = 2 if cols % 2048 == 0 else 1
         vmem = pl.BlockSpec(memory_space=pltpu.VMEM)
         anywhere = pl.BlockSpec(memory_space=pl.ANY)
         dma = pltpu.SemaphoreType.DMA

time: 21.4 us -> 21.4 us (level)
  no operation moved by 1% of the time
where the time goes in v4:
time: 21.4 us; the launch traced here: 21.3 us
  Pallas kernels  21.3 us (100%)
    pallas_call x1, Pallas kernels, body(): pl.pallas_call(functools.partial(first_kernel, R, C, chunks), out_shape=(...  17.6 us
    pallas_call x1, Pallas kernels, body(): pl.pallas_call(functools.partial(second_kernel, parts), out_shape=jax.Sha...  3.67 us

profile of v4, /device:TPU:25, one launch (start us, length us, event | category | flops | bytes accessed | tf_op | source)
XLA Modules:
  0.0 21.3 jit_solution(4208545609313824554)
XLA Ops:
  0.0 17.6 %reflect_one.1 = (f32[1024,2048]{1,0:T(8,128)S(1)}, bf16[1024,240]{1,0:T(8,128)(2,1)S(1)}, bf16[240,2048]{1,0:T(8,128)(2,1)S(1)}) custom-call(s32[8]{0:T(128)} %off_hbm.1, f32[1024,2048]{1,0:T(8,128)} %e_hbm.1, f32[8,8,16]{2,1,0:T(8,128)} %refl_hbm.1), custom_call_target="tpu_custom_call" | custom-call | tf_op jit(solution)/shard_map/reflect_one/pallas_call | solution.py:412
  17.6 3.7 %reflect_two.1 = f32[1024,2048]{1,0:T(8,128)} custom-call(f32[1024,2048]{1,0:T(8,128)S(1)} %get-tuple-element.8.e_ref, bf16[1024,240]{1,0:T(8,128)(2,1)S(1)} %get-tuple-element.9.y_ref, bf16[240,2048]{1,0:T(8,128)(2,1)S(1)} %get-tuple-element.10.c_ref), custom_call_target="tpu_custom_call" | custom-call | tf_op jit(solution)/shard_map/reflect_two/pallas_call | solution.py:451

commit v5 on v4

--- a/solution.py
+++ b/solution.py
@@ -16,7 +16,8 @@
 B = 128
 I = S * W
 N = I + 2 * S
-EARLY = 3
+LOADS = 4
+EARLY = 2
 MIB = 1 << 20
 
 
@@ -73,7 +74,7 @@
     down = lax.min(r + 1, R - 1)
     has_up, has_down = r > 0, r < R - 1
     rows, cols = e_ref.shape
-    step = rows // W
+    step = rows // LOADS
     width = cols // CHUNKS
     TOP = CHUNKS - 1
     piece = refl.shape[2]
@@ -95,7 +96,7 @@
     off_copy = pltpu.make_async_copy(off_hbm, off_ref, off_sem)
     off_copy.start()
     loads = []
-    for i in range(W):
+    for i in range(LOADS):
         part = pl.ds(i * step, step)
         loads.append(pltpu.make_async_copy(e_hbm.at[part], e_ref.at[part], e_sem.at[i]))
     for load in loads[:EARLY]:
@@ -109,7 +110,7 @@
     sends = []
     for d in sorted(range(1, C), key=lambda d: abs(d - C // 2)):
         sends.append(pltpu.make_async_remote_copy(
-            src_ref=mine, dst_ref=gat.at[c], send_sem=out_sem.at[d], recv_sem=gat_sem.at[c],
+            src_ref=mine, dst_ref=gat.at[c], send_sem=out_sem, recv_sem=gat_sem,
             device_id=(r, lax.rem(c + d, C)), device_id_type=MESH))
     for copy in sends:
         copy.start()
@@ -131,7 +132,12 @@
         at = pl.ds(j * width, width)
         return pltpu.make_async_remote_copy(
             src_ref=(top_ref, low_ref)[i].at[:, at], dst_ref=recv.at[i, :, at],
-            send_sem=p_sem.at[i, j], recv_sem=recv_sem.at[i, j],
+            send_sem=p_sem.at[i], recv_sem=recv_sem.at[i, j],
+            device_id=(to, c), device_id_type=MESH)
+
+    def sums_sent(i, to):
+        return pltpu.make_async_remote_copy(
+            src_ref=(top_ref, low_ref)[i], dst_ref=recv.at[i], send_sem=p_sem.at[i], recv_sem=recv_sem.at[i, 0],
             device_id=(to, c), device_id_type=MESH)
 
     @pl.when(r == 0)
@@ -147,7 +153,7 @@
 
     vt[...] = jnp.zeros_like(vt)
 
-    @pl.loop(0, W)
+    @pl.loop(0, LOADS)
     def _(i):
         part = pl.ds(pl.multiple_of(i * step, step), step)
         pltpu.make_async_copy(e_hbm.at[part], e_ref.at[part], e_sem.at[i]).wait()
@@ -159,11 +165,10 @@
     lane = lax.broadcasted_iota(jnp.int32, (S, B), 1)
     sub = lax.broadcasted_iota(jnp.int32, (S, B), 0)
 
-    for d in range(1, C):
-        src = lax.rem(c + d, C)
-        pltpu.make_async_remote_copy(
-            src_ref=mine, dst_ref=gat.at[src], send_sem=out_sem.at[d], recv_sem=gat_sem.at[src],
-            device_id=(r, src), device_id_type=MESH).wait_recv()
+    everyone = pltpu.make_async_remote_copy(
+        src_ref=gat.at[0:C - 1], dst_ref=gat.at[0:C - 1], send_sem=out_sem, recv_sem=gat_sem,
+        device_id=(r, lax.rem(c + 1, C)), device_id_type=MESH)
+    everyone.wait_recv()
 
     parts = [gat[q] for q in range(C)]
     blocks = [(lane >= q * piece) & (lane < (q + 1) * piece) for q in range(C)]
@@ -365,21 +370,18 @@
         c_ref[N + I:2 * N, at] = lo
         c_ref[2 * N + I:3 * N, at] = hi
 
-    for copy in sends:
-        copy.wait_send()
+    everyone.wait_send()
 
     @pl.when(has_up)
     def _():
         msg_copy(0, up).wait_send()
-        for j in range(CHUNKS):
-            sum_copy(0, j, up).wait_send()
+        sums_sent(0, up).wait_send()
 
     @pl.when(has_down)
     def _():
         edge_copy(down).wait_send()
         msg_copy(1, down).wait_send()
-        for j in range(CHUNKS):
-            sum_copy(1, j, down).wait_send()
+        sums_sent(1, down).wait_send()
 
 
 def second_kernel(parts, e_ref, y_ref, c_ref, o_hbm, buf, sem):
@@ -387,7 +389,7 @@
 
     def store(j):
         at = pl.ds(pl.multiple_of(j * width, width), width)
-        return pltpu.make_async_copy(buf.at[:, at], o_hbm.at[:, at], sem.at[j])
+        return pltpu.make_async_copy(buf.at[:, at], o_hbm.at[:, at], sem)
 
     @pl.loop(0, parts)
     def _(j):
@@ -395,9 +397,7 @@
         buf[:, at] = e_ref[:, at] - jnp.dot(y_ref[...], c_ref[:, at], preferred_element_type=F32)
         store(j).start()
 
-    @pl.loop(0, parts)
-    def _(j):
-        store(j).wait()
+    pltpu.make_async_copy(buf, o_hbm, sem).wait()
 
 
 def solution(mesh):
@@ -435,8 +435,8 @@
                 pltpu.VMEM((2, S, B), F32),
                 pltpu.VMEM((2, S, B), F32),
                 pltpu.VMEM((2, S, cols), F32),
-                dma, dma, dma((W,)), dma((C,)), dma((C,)), dma, dma,
-                dma((2,)), dma((2,)), dma((2, chunks)), dma((2, chunks)),
+                dma, dma, dma((LOADS,)), dma, dma, dma, dma,
+                dma((2,)), dma((2,)), dma((2,)), dma((2, chunks)),
             ],
             compiler_params=pltpu.CompilerParams(
                 collective_id=0, has_side_effects=True, vmem_limit_bytes=24 * MIB
@@ -453,7 +453,7 @@
             out_shape=jax.ShapeDtypeStruct((rows, cols), F32),
             in_specs=[vmem, vmem, vmem],
             out_specs=anywhere,
-            scratch_shapes=[pltpu.VMEM((rows, cols), F32), dma((parts,))],
+            scratch_shapes=[pltpu.VMEM((rows, cols), F32), dma],
             compiler_params=pltpu.CompilerParams(vmem_limit_bytes=16 * MIB),
             name="reflect_two",
         )(*(pltpu.with_memory_space_constraint(x, pltpu.VMEM) for x in (e, y, coeff)))

time: 21.4 us -> 21.1 us (0.986)
  Pallas kernels: 21.3 us -> 21 us
where the time goes in v5:
time: 21.1 us; the launch traced here: 21 us
  Pallas kernels  21 us (100%)
    pallas_call x1, Pallas kernels, body(): pl.pallas_call(functools.partial(first_kernel, R, C, chunks), out_shape=(...  17.4 us
    pallas_call x1, Pallas kernels, body(): pl.pallas_call(functools.partial(second_kernel, parts), out_shape=jax.Sha...  3.61 us

profile of v5, /device:TPU:25, one launch (start us, length us, event | category | flops | bytes accessed | tf_op | source)
XLA Modules:
  0.0 21.0 jit_solution(662446603980591459)
XLA Ops:
  0.0 17.4 %reflect_one.1 = (f32[1024,2048]{1,0:T(8,128)S(1)}, bf16[1024,240]{1,0:T(8,128)(2,1)S(1)}, bf16[240,2048]{1,0:T(8,128)(2,1)S(1)}) custom-call(s32[8]{0:T(128)} %off_hbm.1, f32[1024,2048]{1,0:T(8,128)} %e_hbm.1, f32[8,8,16]{2,1,0:T(8,128)} %refl_hbm.1), custom_call_target="tpu_custom_call" | custom-call | tf_op jit(solution)/shard_map/reflect_one/pallas_call | solution.py:412
  17.4 3.6 %reflect_two.1 = f32[1024,2048]{1,0:T(8,128)} custom-call(f32[1024,2048]{1,0:T(8,128)S(1)} %get-tuple-element.8.e_ref, bf16[1024,240]{1,0:T(8,128)(2,1)S(1)} %get-tuple-element.9.y_ref, bf16[240,2048]{1,0:T(8,128)(2,1)S(1)} %get-tuple-element.10.c_ref), custom_call_target="tpu_custom_call" | custom-call | tf_op jit(solution)/shard_map/reflect_two/pallas_call | solution.py:451

commit v6 on v5

--- a/solution.py
+++ b/solution.py
@@ -80,16 +80,16 @@
     piece = refl.shape[2]
 
     barrier = pltpu.get_barrier_semaphore()
+    @pl.when(has_up)
+    def _():
+        pl.semaphore_signal(barrier, inc=1, device_id=(up, c), device_id_type=MESH)
+
+    @pl.when(has_down)
+    def _():
+        pl.semaphore_signal(barrier, inc=1, device_id=(down, c), device_id_type=MESH)
+
     for d in range(1, C):
         pl.semaphore_signal(barrier, inc=1, device_id=(r, lax.rem(c + d, C)), device_id_type=MESH)
-
-    @pl.when(has_up)
-    def _():
-        pl.semaphore_signal(barrier, inc=1, device_id=(up, c), device_id_type=MESH)
-
-    @pl.when(has_down)
-    def _():
-        pl.semaphore_signal(barrier, inc=1, device_id=(down, c), device_id_type=MESH)
 
     refl_copy = pltpu.make_async_copy(refl_hbm, refl, refl_sem)
     refl_copy.start()
@@ -237,14 +237,16 @@
             u, lambda s, t: coef[0, pair_index(s, t)], lambda s, t: coef[1, pair_index(s, t)],
             lambda s, t: coef[2, pair_index(s, t)], lambda s: fact[s], w)
 
+    off = jnp.zeros((S, B), jnp.int32)
+    for s in range(S):
+        off = jnp.where(sub == s, off_ref[s], off)
+    firsts = [row_of(heres[s], 0) for s in range(S)]
+
     def top_part():
         @pl.when(has_up)
         def _():
             edge_copy(up).wait_recv()
 
-        off = jnp.zeros((S, B), jnp.int32)
-        for s in range(S):
-            off = jnp.where(sub == s, off_ref[s], off)
         x = top[...]
         tau_top = jnp.where(has_up, 2.0 / (lane_sum(x * x) + EPS), 0.0)
         x = jnp.where(lane < off, x, 0.0)
@@ -253,7 +255,7 @@
         vt[N + I:2 * N, 0:B] = lo
         vt[2 * N + I:3 * N, 0:B] = hi
         first = gather_rows(heres, 0)
-        into = [jnp.where(sub > s, lane_sum(x * row_of(heres[s], 0)), 0.0) for s in range(S)]
+        into = [jnp.where(sub > s, lane_sum(x * firsts[s]), 0.0) for s in range(S)]
         meet = jnp.zeros((S, B), F32)
         tops = jnp.zeros((S, B), F32)
         for t in range(S):

time: 21.1 us -> 21.1 us (level)
  no operation moved by 1% of the time
where the time goes in v6:
time: 21.1 us; the launch traced here: 21 us
  Pallas kernels  21 us (100%)
    pallas_call x1, Pallas kernels, body(): pl.pallas_call(functools.partial(first_kernel, R, C, chunks), out_shape=(...  17.4 us
    pallas_call x1, Pallas kernels, body(): pl.pallas_call(functools.partial(second_kernel, parts), out_shape=jax.Sha...  3.61 us

profile of v6, /device:TPU:25, one launch (start us, length us, event | category | flops | bytes accessed | tf_op | source)
XLA Modules:
  0.0 21.0 jit_solution(4383551814950189285)
XLA Ops:
  0.0 17.4 %reflect_one.1 = (f32[1024,2048]{1,0:T(8,128)S(1)}, bf16[1024,240]{1,0:T(8,128)(2,1)S(1)}, bf16[240,2048]{1,0:T(8,128)(2,1)S(1)}) custom-call(s32[8]{0:T(128)} %off_hbm.1, f32[1024,2048]{1,0:T(8,128)} %e_hbm.1, f32[8,8,16]{2,1,0:T(8,128)} %refl_hbm.1), custom_call_target="tpu_custom_call" | custom-call | tf_op jit(solution)/shard_map/reflect_one/pallas_call | solution.py:414
  17.4 3.6 %reflect_two.1 = f32[1024,2048]{1,0:T(8,128)} custom-call(f32[1024,2048]{1,0:T(8,128)S(1)} %get-tuple-element.8.e_ref, bf16[1024,240]{1,0:T(8,128)(2,1)S(1)} %get-tuple-element.9.y_ref, bf16[240,2048]{1,0:T(8,128)(2,1)S(1)} %get-tuple-element.10.c_ref), custom_call_target="tpu_custom_call" | custom-call | tf_op jit(solution)/shard_map/reflect_two/pallas_call | solution.py:453
